TPU v7x, 32 devices: a whole 2x2x4 slice. The times are simulated.
32 devices in a mesh: groups: 2 (over y), tensor: 8 (over z, x), context: 2 (over core).
Axes of the slice: x: 2, y: 2, z: 4, core: 2. Of those that a mesh axis runs over, the one named last changes fastest.
Arguments:
- activations: bfloat16 [16384, 28672], P(('groups', 'context'), 'tensor'), parts along dimension 0, may hold values from -6 to 6
- out_grads: bfloat16 [16384, 8192], P(('groups', 'context'), 'tensor'), parts along dimension 0, may hold values from -6 to 6
- basis_in: bfloat16 [28672, 64], P('tensor'), may hold values from -0.03125 to 0.03125
- basis_out: bfloat16 [8192, 64], P('tensor'), may hold values from -0.0625 to 0.0625
- val_sketches: bfloat16 [512, 4096], P('tensor'), may hold values from -0.01171875 to 0.01171875
- val_owner: int32 [512], P('tensor'), may hold values from 0 to 511, each once
- example_ids: int32 [256], P(('groups', 'context')), parts along dimension 0, may hold values from 0 to 63, never falling along the last dimension, each value on 1 to 4 neighbouring positions
Outputs:
- sketches: bfloat16 [128, 4096], P('groups'), parts along dimension 0
- scores: float32 [128, 512], P('groups', 'tensor'), parts along dimension 0
There are 2 independent parts, one for each index of `groups`. A program takes and returns all parts, laid end to end along the dimension named above; an argument that names none is the same for every part. Nothing has to cross between parts.
Inputs may be any that keep to these rules, and one draw needn't show every extreme that they name: `val_owner`: a permutation of the stored rows. `example_ids`: never falling along the sequence; each example covers 1 to 4 blocks, one exactly 4; every example is present.
All inputs are finite; a program needn't handle non-finite values.
Results may differ from a plain program's by a relative error of at most 0.0059.
Values may be sent and summed in bfloat16 or wider, within the bound.
A program may use at most 128 MiB of HBM per device.

v0:
```python
import jax
import jax.numpy as jnp
from jax import lax
from jax.sharding import PartitionSpec as P


def per_device(activations, out_grads, basis_in, basis_out, val_sketches, val_owner, example_ids):
    rank = basis_in.shape[1]
    tokens = activations.shape[0]
    nblock = example_ids.shape[0]
    block = tokens // nblock
    examples = nblock * lax.axis_size("context") // 2
    labels = jnp.arange(examples, dtype=jnp.int32)
    local = jnp.concatenate(
        [
            jnp.dot(activations, basis_in, preferred_element_type=jnp.float32),
            jnp.dot(out_grads, basis_out, preferred_element_type=jnp.float32),
        ],
        axis=1,
    )
    total = lax.psum(local, "tensor")
    proj_in = total[:, :rank].astype(jnp.bfloat16).reshape(nblock, block, rank)
    proj_out = total[:, rank:].astype(jnp.bfloat16).reshape(nblock, block, rank)
    outer = jnp.einsum(
        "kta,ktb->kab", proj_in, proj_out, preferred_element_type=jnp.float32
    ).reshape(nblock, rank * rank)
    member = (example_ids[:, None] == labels[None, :]).astype(jnp.float32)
    partial_sk = lax.dot_general(
        member, outer, (((0,), (0,)), ((), ())), precision=lax.Precision.HIGHEST
    )
    summed = lax.psum(partial_sk.astype(jnp.bfloat16), "context")
    piece = lax.all_gather(val_sketches, "tensor", axis=0, tiled=True)
    count = piece.shape[0]
    select = (val_owner[:, None] == jnp.arange(count, dtype=jnp.int32)[None, :]).astype(
        jnp.bfloat16
    )
    chosen = jnp.dot(select, piece, preferred_element_type=jnp.float32).astype(jnp.bfloat16)
    scores = lax.dot_general(
        summed, chosen, (((1,), (1,)), ((), ())), preferred_element_type=jnp.float32
    )
    return (summed, scores)


def solution(mesh):
    return jax.shard_map(
        per_device,
        mesh=mesh,
        in_specs=(
            P(("groups", "context"), "tensor"),
            P(("groups", "context"), "tensor"),
            P("tensor", None),
            P("tensor", None),
            P("tensor", None),
            P("tensor"),
            P(("groups", "context")),
        ),
        out_specs=(P("groups", None), P("groups", "tensor")),
        check_vma=False,
    )
```

profile of v0, /device:TPU:1, one launch (start us, length us, event | category | flops | bytes accessed | tf_op | source)
XLA Modules:
  0.0 221.8 jit_solution(16252792757408522412)
XLA Ops:
  8.0 0.0 copy-start
  8.0 0.0 copy-start.2
  8.0 0.0 all-reduce.3.cloned.1.call-start
  8.1 1.0 copy-done
  9.0 14.2 %fusion.7 = f32[4096,64]{0,1:T(8,128)S(1)} fusion(bf16[4096,3584]{1,0:T(8,128)(2,1)} %param.7, bf16[3584,64]{0,1:T(8,128)(2,1)S(1)} %copy-done), kind=kOutput, calls=%fused_computation.11 | convolution fusion | flops 1879048192 | bytes 30867456 | tf_op jit(solution)/shard_map/dot_general | solution.py:16
  23.2 0.0 copy-done.2
  23.2 6.0 %fusion.8 = f32[4096,64]{0,1:T(8,128)S(1)} fusion(bf16[4096,1024]{1,0:T(8,128)(2,1)} %param.8, bf16[1024,64]{0,1:T(8,128)(2,1)S(1)} %copy-done.2), kind=kOutput, calls=%fused_computation.12 | convolution fusion | flops 536870912 | bytes 9568256 | tf_op jit(solution)/shard_map/dot_general | solution.py:17
  29.3 0.2 pad_maximum_fusion
  29.4 84.8 %all-reduce.4 = bf16[4096,128]{0,1:T(8,128)(2,1)} all-reduce(f32[4096,128]{0,1:T(8,128)S(1)} %pad_maximum_fusion), channel_id=1, replica_groups=mesh['groups'=2,'tensor'=8,'context'=2] {'tensor'}, use_global_device_ids=true, to_apply=%region_0.0 | all-reduce | flops 524288 | bytes 3145728 | tf_op jit(solution)/shard_map/psum | solution.py:21
  114.2 1.3 fusion.6
  115.5 1.3 copy.11
  116.8 2.2 reshape.15
  119.0 2.5 %fusion.1 = f32[64,64,64]{2,1,0:T(8,128)S(1)} fusion(bf16[64,64,64]{2,1,0:T(8,128)(2,1)} %bitcast.11, bf16[64,64,64]{1,0,2:T(8,128)(2,1)} %reshape.15), kind=kOutput, calls=%fused_computation.4 | convolution fusion | flops 33554432 | bytes 2097152 | tf_op jit(solution)/shard_map/kta,ktb->kab/dot_general | solution.py:24
  121.4 1.6 reshape.17
  123.1 0.0 copy-done.3
  123.1 2.7 %convolution_convert_fusion.1 = bf16[64,4096]{1,0:T(8,128)(2,1)} fusion(f32[64,4096]{1,0:T(8,128)} %reshape.17, s32[64]{0:T(128)S(1)} %copy-done.3), kind=kOutput, calls=%fused_computation.1 | convolution fusion | flops 201592832 | bytes 1573120 | tf_op jit(solution)/shard_map/dot_general | solution.py:28
  125.8 0.0 all-reduce.3.cloned.1.call-update
  125.8 0.0 all-gather.2.cloned.1.call-start
  125.8 0.5 all-gather.2.cloned.1.call-update
  126.4 27.7 %all-reduce.3.cloned.1.call-done = bf16[64,4096]{1,0:T(8,128)(2,1)} async-done(((bf16[64,4096]{1,0:T(8,128)(2,1)}), bf16[64,4096]{1,0:T(8,128)(2,1)}) %all-reduce.3.cloned.1.call-update) | async-done | bytes 524304 | tf_op jit(solution)/shard_map/psum | solution.py:31
  154.1 55.3 %all-gather.2.cloned.1.call-done = bf16[512,4096]{1,0:T(8,128)(2,1)} async-done(((bf16[64,4096]{1,0:T(8,128)(2,1)}), bf16[512,4096]{1,0:T(8,128)(2,1)}) %all-gather.2.cloned.1.call-update) | async-done | bytes 4194320 | tf_op jit(solution)/shard_map/all_gather | solution.py:32
  209.4 4.1 %fusion = f32[64,64]{1,0:T(8,128)} fusion(bf16[64,4096]{1,0:T(8,128)(2,1)} %all-reduce.3.cloned.1.call-done, bf16[512,4096]{1,0:T(8,128)(2,1)} %all-gather.2.cloned.1.call-done, s32[64]{0:T(128)S(1)} %copy-done.4), kind=kOutput, calls=%fused_computation.3 | convolution fusion | flops 302284800 | bytes 4735232 | tf_op jit(solution)/shard_map/dot_general | solution.py:38
  213.5 0.0 copy-done.1
  213.5 0.8 copy.17
  (4 shorter events, 0.0 us)
Async XLA Ops:
  8.0 1.0 copy-start
  8.0 15.2 %copy-start.2 = (bf16[1024,64]{0,1:T(8,128)(2,1)S(1)}, bf16[1024,64]{0,1:T(8,128)(2,1)}, u32[]{:S(2)}) copy-start(bf16[1024,64]{0,1:T(8,128)(2,1)} %param.10) | copy-start | bytes 393220
  8.0 146.1 %all-reduce.3.cloned.1.call-start = ((), (), s32[]{:S(2)}) async-start(), calls=%async_computation | async-start | bytes 1048576 | tf_op jit(solution)/shard_map/psum | solution.py:31
  116.8 6.3 %copy-start.3 = (s32[64]{0:T(128)S(1)}, s32[64]{0:T(128)}, u32[]{:S(2)}) copy-start(s32[64]{0:T(128)} %param.13) | copy-start | bytes 772
  119.0 90.5 %copy-start.4 = (s32[64]{0:T(128)S(1)}, s32[64]{0:T(128)}, u32[]{:S(2)}) copy-start(s32[64]{0:T(128)} %param.12) | copy-start | bytes 772
  125.8 83.6 %all-gather.2.cloned.1.call-start = ((), (), s32[]{:S(2)}) async-start(), calls=%async_computation.1 | async-start | bytes 4718592 | tf_op jit(solution)/shard_map/all_gather | solution.py:32
  154.1 59.5 %copy-start.1 = (bf16[64,4096]{1,0:T(8,128)(2,1)S(1)}, bf16[64,4096]{1,0:T(8,128)(2,1)}, u32[]{:S(2)}) copy-start(bf16[64,4096]{1,0:T(8,128)(2,1)} %all-reduce.3.cloned.1.call-done) | copy-start | bytes 1572868
Sparse Core Ops, SparseCore 0:
  125.9 28.1 all-reduce.2
Sparse Core Ops, SparseCore 1:
  128.6 80.8 all-gather.1
where the time goes:
time: 224 us; the launch traced here: 222 us
  blocking collectives  84.8 us (38%)
  waiting for transfers between devices  83.6 us (37%)
  matrix products  29.5 us (13%)
  between operations  15.5 us (7%)
  local copies, waits for them, and re-layouts  8.13 us (4%)
    psum x1, blocking collectives, per_device(): total = lax.psum(local, 'tensor')  84.8 us
    all_gather x1, waiting for transfers between devices, per_device(): piece = lax.all_gather(val_sketches, 'tensor', axis=0, tiled=True)  55.3 us
    psum x1, waiting for transfers between devices, per_device(): summed = lax.psum(partial_sk.astype(jnp.bfloat16), 'context')  27.7 us
    dot_general x1, matrix products, per_device(): jnp.dot(activations, basis_in, preferred_element_type=jnp.float32)  14.2 us
    dot_general x1, matrix products, per_device(): jnp.dot(out_grads, basis_out, preferred_element_type=jnp.float32)  6.04 us
  transfers between devices with their start and end apart: 2, of which 2 were waited for; matrix products, arithmetic and copies ran while one was open for 0% of the time, Pallas kernels for 0%

commit v1 on v0

v1 whole, which is shorter than its diff:
```python
import functools

import jax
import jax.numpy as jnp
from jax import lax
from jax.experimental import pallas as pl
from jax.experimental.pallas import tpu as pltpu
from jax.sharding import PartitionSpec as P

MESH = pl.DeviceIdType.MESH
F32, BF16 = jnp.float32, jnp.bfloat16
BUFFERS = 3


def one_hot(rows, columns, hit):
    row = lax.broadcasted_iota(jnp.int32, (rows, columns), 0)
    column = lax.broadcasted_iota(jnp.int32, (rows, columns), 1)
    return jnp.where(hit(row, column), 1.0, 0.0).astype(BF16)


def kernel(
    size, slots, act, grads, basis_in, basis_out, val, owner, ids, sketches, scores,
    abuf, gbuf, wide_in, wide_out, sent, xbuf, zbuf, acc, terms, firsts, held, pieces,
    act_sem, grad_sem, x_send, x_recv, z_send, z_recv, first_send, first_recv,
    gx_send, gz_send, gc_send, g_recv, s_send, s_recv,
):
    c = lax.axis_index("context")
    t = lax.axis_index("tensor")
    half = size // 2
    rows = acc.shape[0]
    rank = basis_in.shape[1]
    examples = sketches.shape[0]
    parity, mine = t % 2, t // 2
    pair = t + 1 - 2 * parity
    other = 1 - c
    nblock = ids.shape[0]
    block = rows * size // nblock

    def peer(j):
        return (mine + 1 + j) % half

    def target(i):
        side = jnp.where(i < half, 1 - parity, parity)
        return 2 * peer(i % half) + side

    def load(i):
        slot = i % BUFFERS
        start = pl.multiple_of(target(i) * rows, rows)
        return (
            pltpu.make_async_copy(act.at[pl.ds(start, rows), :], abuf.at[slot], act_sem.at[slot]),
            pltpu.make_async_copy(grads.at[pl.ds(start, rows), :], gbuf.at[slot], grad_sem.at[slot]),
        )

    def begin(i):
        for copy in load(i):
            copy.start()

    for i in range(BUFFERS - 1):
        begin(i)

    barrier = pltpu.get_barrier_semaphore()

    def greet(j, carry):
        pl.semaphore_signal(barrier, inc=1, device_id={"tensor": (t + 1 + j) % size}, device_id_type=MESH)
        return carry

    lax.fori_loop(0, size - 1, greet, 0)
    pl.semaphore_signal(barrier, inc=1, device_id={"context": other}, device_id_type=MESH)

    wide_in[...] = jnp.zeros_like(wide_in)
    wide_out[...] = jnp.zeros_like(wide_out)
    wide_in[:, :rank] = basis_in[...]
    wide_out[:, rank:] = basis_out[...]

    lanes = firsts.shape[2]
    lane = lax.broadcasted_iota(jnp.int32, (8, lanes), 1)

    def first(j, vector):
        return jnp.where(lane // (2 * slots) == j, ids[(j * rows) // block], vector)

    firsts[c] = lax.fori_loop(0, size, first, jnp.zeros((8, lanes), jnp.int32))
    pl.semaphore_wait(barrier, size)

    def share_firsts(index):
        return pltpu.make_async_remote_copy(
            src_ref=firsts.at[index], dst_ref=firsts.at[index], send_sem=first_send, recv_sem=first_recv,
            device_id={"context": other}, device_id_type=MESH,
        )

    share_firsts(c).start()

    def project(i):
        slot = i % BUFFERS
        for copy in load(i):
            copy.wait()

        @pl.when(i + BUFFERS - 1 < size)
        def _():
            begin(i + BUFFERS - 1)

        return jnp.dot(abuf[slot], wide_in[...], preferred_element_type=F32) + jnp.dot(
            gbuf[slot], wide_out[...], preferred_element_type=F32
        )

    def across(k):
        return pltpu.make_async_remote_copy(
            src_ref=sent.at[k], dst_ref=xbuf.at[k], send_sem=x_send.at[k], recv_sem=x_recv.at[k],
            device_id={"tensor": pair}, device_id_type=MESH,
        )

    def along(k, slot):
        return pltpu.make_async_remote_copy(
            src_ref=sent.at[half + k], dst_ref=zbuf.at[slot], send_sem=z_send.at[k], recv_sem=z_recv.at[slot],
            device_id={"tensor": 2 * k + parity}, device_id_type=MESH,
        )

    def first_half(i, carry):
        k = peer(i)
        sent[k] = project(i).astype(BF16)
        across(k).start()
        return carry

    lax.fori_loop(0, half, first_half, 0)

    def second_half(i, carry):
        k = peer(i)
        value = project(half + i)
        across(k).wait_recv()
        value = value + xbuf[k].astype(F32)
        acc[...] = value

        @pl.when(i < half - 1)
        def _():
            sent[half + k] = value.astype(BF16)
            along(k, mine).start()

        return carry

    lax.fori_loop(0, half, second_half, 0)

    def collect(j, carry):
        k = peer(j)
        along(k, k).wait_recv()
        acc[...] += zbuf[k].astype(F32)
        return carry

    lax.fori_loop(0, half - 1, collect, 0)

    proj = acc[...].astype(BF16)
    pick = one_hot(2 * rank, rank, lambda r, q: r == 2 * (q % (rank // 2)) + q // (rank // 2))
    twice = one_hot(2 * rank, 2 * rank, lambda r, q: r == rank + q % rank)
    left = jnp.dot(proj, pick, preferred_element_type=F32).astype(BF16)
    right = jnp.dot(proj, twice, preferred_element_type=F32).astype(BF16)
    deep = rank // 2
    part = min(block, rows)
    count = rows // part
    low = lax.broadcasted_iota(jnp.int32, (deep, 2 * rank), 1) < rank
    outers = []
    for k in range(count):
        o = lax.dot_general(
            left[k * part:(k + 1) * part], right[k * part:(k + 1) * part], (((0,), (0,)), ((), ())),
            preferred_element_type=F32,
        )
        outers.append(jnp.where(low, o[:deep], o[deep:]))
    start = (t * rows) // block
    offsets = [ids[start + k] - ids[start] for k in range(count)]
    for s in range(slots):
        total = jnp.zeros((deep, 2 * rank), F32)
        for k in range(count):
            total = total + outers[k] * jnp.where(offsets[k] == s, 1.0, 0.0)
        terms[s * deep:(s + 1) * deep, :] = total
    me = c * size + t
    width = deep // 2
    for a in range(width):
        value = jnp.concatenate(
            [terms[pl.ds(a, slots, stride=deep), :], terms[pl.ds(width + a, slots, stride=deep), :]], axis=0
        )
        held[me, :, a * 2 * rank:(a + 1) * 2 * rank] = value.astype(BF16)

    def give(index, send_sem, device):
        return pltpu.make_async_remote_copy(
            src_ref=held.at[index], dst_ref=held.at[index], send_sem=send_sem, recv_sem=g_recv.at[index],
            device_id=device, device_id_type=MESH,
        )

    def to_peer(k):
        return give(me, gz_send.at[k], {"tensor": 2 * k + parity})

    def to_pair(k):
        return give(c * size + 2 * k + parity, gx_send.at[k], {"tensor": pair})

    def to_core(k):
        return give(c * size + k, gc_send.at[k], {"context": other})

    def arrived(index):
        give(index, gc_send.at[0], {"context": other}).wait_recv()

    def loop(n, body):
        def step(j, carry):
            body(j)
            return carry

        lax.fori_loop(0, n, step, 0)

    loop(half - 1, lambda j: to_peer(peer(j)).start())
    to_pair(mine).start()
    to_core(t).start()

    def from_peer(j):
        k = peer(j)
        arrived(c * size + 2 * k + parity)
        to_pair(k).start()
        to_core(2 * k + parity).start()

    loop(half - 1, from_peer)

    def from_pair(j):
        k = 2 * peer(half - 1 + j) + 1 - parity
        arrived(c * size + k)
        to_core(k).start()

    loop(half, from_pair)
    share_firsts(other).wait_recv()
    loop(size, lambda k: arrived(other * size + k))

    wide = held.shape[2]
    chosen = []
    for core in range(2):
        row = lax.broadcasted_iota(jnp.int32, (2 * examples, lanes), 0)
        column = lax.broadcasted_iota(jnp.int32, (2 * examples, lanes), 1)
        at = firsts[core, 0:1, :] + column % slots
        hit = (row % examples == at) & (row // examples == column // slots % 2)
        chosen.append(jnp.where(hit, 1.0, 0.0).astype(BF16))
    tile = min(512, wide)
    for p in range(wide // tile):
        total = jnp.zeros((2 * examples, tile), F32)
        for core in range(2):
            data = held[core * size:(core + 1) * size, :, p * tile:(p + 1) * tile]
            total = total + jnp.dot(chosen[core], data.reshape(lanes, tile), preferred_element_type=F32)
        total = total.astype(BF16)
        sketches[:, p * tile:(p + 1) * tile] = total[:examples]
        sketches[:, wide + p * tile:wide + (p + 1) * tile] = total[examples:]

    local = lax.dot_general(
        val[...], sketches[...], (((1,), (1,)), ((), ())), preferred_element_type=F32
    )
    depth = pieces.shape[1]
    pieces[t] = jnp.concatenate([local[:depth], local[depth:]], axis=1)

    def send_scores(k, slot):
        return pltpu.make_async_remote_copy(
            src_ref=pieces.at[t], dst_ref=pieces.at[slot], send_sem=s_send.at[k], recv_sem=s_recv.at[slot],
            device_id={"tensor": k}, device_id_type=MESH,
        )

    loop(size - 1, lambda j: send_scores((t + 1 + j) % size, t).start())

    def got(j):
        k = (t + 1 + j) % size
        send_scores(k, k).wait_recv()

    loop(size - 1, got)
    table = pieces[...].reshape(size * depth, 2 * examples)
    result = jnp.zeros(scores.shape, F32)
    hots = [
        jnp.where(
            lax.broadcasted_iota(jnp.int32, (size * depth, scores.shape[1]), 0) // depth * (2 * depth)
            + h * depth
            + lax.broadcasted_iota(jnp.int32, (size * depth, scores.shape[1]), 0) % depth
            == owner[...],
            1.0, 0.0,
        ).astype(BF16)
        for h in range(2)
    ]
    for _ in range(3):
        digit = table.astype(BF16)
        table = table - digit.astype(F32)
        for h in range(2):
            result = result + lax.dot_general(
                digit[:, h * examples:(h + 1) * examples], hots[h], (((0,), (0,)), ((), ())),
                preferred_element_type=F32,
            )
    scores[...] = result

    share_firsts(c).wait_send()
    loop(half, lambda k: across(k).wait_send())
    loop(half - 1, lambda j: along(peer(j), mine).wait_send())
    loop(half - 1, lambda j: to_peer(peer(j)).wait_send())
    loop(half, lambda k: to_pair(k).wait_send())
    loop(size, lambda k: to_core(k).wait_send())
    loop(size - 1, lambda j: send_scores((t + 1 + j) % size, t).wait_send())


def per_device(activations, out_grads, basis_in, basis_out, val_sketches, val_owner, example_ids):
    size = lax.axis_size("tensor")
    tokens, deep_in = activations.shape
    deep_out = out_grads.shape[1]
    rank = basis_in.shape[1]
    nblock = example_ids.shape[0]
    examples = nblock * lax.axis_size("context") // 2
    rows = tokens // size
    half = size // 2
    slots = max(8, rows // (tokens // nblock))
    stored, width = val_sketches.shape
    depth = max(8, stored // 2)
    if 2 * depth != stored:
        val_sketches = jnp.pad(val_sketches, ((0, 2 * depth - stored), (0, 0)))
        val_owner_at = val_owner // stored * (2 * depth) + val_owner % stored
    else:
        val_owner_at = val_owner
    vmem = pl.BlockSpec(memory_space=pltpu.VMEM)
    hbm = pl.BlockSpec(memory_space=pl.ANY)
    dma = pltpu.SemaphoreType.DMA
    return pl.pallas_call(
        functools.partial(kernel, size, slots),
        out_shape=(
            jax.ShapeDtypeStruct((examples, width), BF16),
            jax.ShapeDtypeStruct((examples, stored), F32),
        ),
        in_specs=[hbm, hbm, vmem, vmem, vmem, vmem, pl.BlockSpec(memory_space=pltpu.SMEM)],
        out_specs=(vmem, vmem),
        scratch_shapes=[
            pltpu.VMEM((BUFFERS, rows, deep_in), BF16),
            pltpu.VMEM((BUFFERS, rows, deep_out), BF16),
            pltpu.VMEM((deep_in, 2 * rank), BF16),
            pltpu.VMEM((deep_out, 2 * rank), BF16),
            pltpu.VMEM((size, rows, 2 * rank), BF16),
            pltpu.VMEM((half, rows, 2 * rank), BF16),
            pltpu.VMEM((half, rows, 2 * rank), BF16),
            pltpu.VMEM((rows, 2 * rank), F32),
            pltpu.VMEM((slots * rank // 2, 2 * rank), F32),
            pltpu.VMEM((2, 8, size * 2 * slots), jnp.int32),
            pltpu.VMEM((2 * size, 2 * slots, width // 2), BF16),
            pltpu.VMEM((size, depth, 2 * examples), F32),
            dma((BUFFERS,)), dma((BUFFERS,)),
            dma((half,)), dma((half,)), dma((half,)), dma((half,)),
            dma, dma,
            dma((half,)), dma((half,)), dma((size,)), dma((2 * size,)),
            dma((size,)), dma((size,)),
        ],
        compiler_params=pltpu.CompilerParams(
            collective_id=0, has_side_effects=True, vmem_limit_bytes=48 * 1024 * 1024
        ),
        cost_estimate=pl.CostEstimate(
            flops=2 * tokens * (deep_in + deep_out) * rank,
            bytes_accessed=2 * tokens * (deep_in + deep_out),
            transcendentals=0,
        ),
    )(activations, out_grads, basis_in, basis_out, val_sketches, val_owner_at.reshape(1, stored), example_ids)


def solution(mesh):
    return jax.shard_map(
        per_device,
        mesh=mesh,
        in_specs=(
            P(("groups", "context"), "tensor"),
            P(("groups", "context"), "tensor"),
            P("tensor", None),
            P("tensor", None),
            P("tensor", None),
            P("tensor"),
            P(("groups", "context")),
        ),
        out_specs=(P("groups", None), P("groups", "tensor")),
        check_vma=False,
    )
```

time: 224 us -> 52 us (0.23)
  blocking collectives: 84.8 us -> 0 us
  waiting for transfers between devices: 83.6 us -> 0 us
  Pallas kernels: 0 us -> 44.9 us
  matrix products: 29.5 us -> 0 us
  between operations: 15.5 us -> 0.66 us
    psum x1 -> x0, blocking collectives: 84.8 us -> none  [per_device(): total = lax.psum(local, 'tensor')]
    all_gather x1 -> x0, waiting for transfers between devices: 55.3 us -> none  [per_device(): piece = lax.all_gather(val_sketches, 'tensor', axis=0, tiled=True)]
    pallas_call x0 -> x1, Pallas kernels: none -> 44.9 us  [per_device(): pl.pallas_call(functools.partial(kernel, size, slots), out_shape=(jax.Sha...]
    dot_general x5 -> x0, matrix products: 29.5 us -> none  [the longest x1 14.2 us: per_device(): jnp.dot(activations, basis_in, preferred_element_type=jnp.float32)]
    psum x1 -> x0, waiting for transfers between devices: 27.7 us -> none  [per_device(): summed = lax.psum(partial_sk.astype(jnp.bfloat16), 'context')]
    reshape x3 -> x0, local copies, waits for them, and re-layouts: 5.09 us -> none  [the longest x1 2.15 us: per_device(): proj_in = total[:, :rank].astype(jnp.bfloat16).reshape(nblock, block, rank)]
    unnamed x11 -> x10, local copies, waits for them, and re-layouts: 1.77 us -> 6.28 us
  transfers between devices with their start and end apart: 2 -> 0, of which waited for: 2 -> 0; matrix products, arithmetic and copies ran while one was open for 0% -> 0% of each run, Pallas kernels for 0% -> 0%
where the time goes in v1:
time: 52 us; the launch traced here: 51.8 us
  Pallas kernels  44.9 us (86%)
  local copies, waits for them, and re-layouts  6.28 us (12%)
  between operations  0.66 us (1%)
    pallas_call x1, Pallas kernels, per_device(): pl.pallas_call(functools.partial(kernel, size, slots), out_shape=(jax.Sha...  44.9 us
    unnamed x10, local copies, waits for them, and re-layouts  6.28 us

profile of v1, /device:TPU:1, one launch (start us, length us, event | category | flops | bytes accessed | tf_op | source)
XLA Modules:
  0.0 51.8 jit_solution(17817609741707742396)
XLA Ops:
  0.6 1.1 %copy.10.basis_out = bf16[1024,64]{1,0:T(8,128)(2,1)S(1)} copy(bf16[1024,64]{0,1:T(8,128)(2,1)} %param.10) | data formatting | bytes 262144 | tf_op args[3]
  1.7 1.4 %copy.9.basis_in = bf16[3584,64]{1,0:T(8,128)(2,1)S(1)} copy(bf16[3584,64]{0,1:T(8,128)(2,1)} %param.9) | data formatting | bytes 917504 | tf_op args[2]
  3.2 0.0 copy-start
  3.2 1.0 %copy-done = bf16[64,4096]{1,0:T(8,128)(2,1)S(1)} copy-done((bf16[64,4096]{1,0:T(8,128)(2,1)S(1)}, bf16[64,4096]{1,0:T(8,128)(2,1)}, u32[]{:S(2)}) %copy-start) | copy-done | bytes 524312
  4.2 0.0 copy-start.1
  4.2 0.7 %copy-done.1 = s32[64]{0:T(128)S(1)} copy-done((s32[64]{0:T(128)S(1)}, s32[64]{0:T(128)}, u32[]{:S(2)}) %copy-start.1) | copy-done | bytes 280
  4.9 0.0 copy-start.2
  4.9 0.7 %copy-done.2 = s32[64]{0:T(128)S(1)} copy-done((s32[64]{0:T(128)S(1)}, s32[64]{0:T(128)}, u32[]{:S(2)}) %copy-start.2) | copy-done | bytes 280
  5.5 44.9 %shard_map.86 = (bf16[64,4096]{1,0:T(8,128)(2,1)S(1)}, f32[64,64]{1,0:T(8,128)S(1)}) custom-call(bf16[4096,3584]{1,0:T(8,128)(2,1)} %act.1, bf16[4096,1024]{1,0:T(8,128)(2,1)} %grads.1, bf16[3584,64]{1,0:T(8,128)(2,1)S(1)} %copy.9.basis_in, bf16[1024,64]{1,0:T(8,128)(2,1)S(1)} %copy.10.basis_out, bf16[64,4096]{1,0:T(8,128)(2,1)S(1)} %copy-done, ...), custom_call_target="tpu_custom_call" | custom-call | flops 2415919104 | bytes 37748736 | tf_op jit(solution)/shard_map/pallas_call | solution.py:314
  50.4 0.8 %copy.13 = bf16[64,4096]{1,0:T(8,128)(2,1)} copy(bf16[64,4096]{1,0:T(8,128)(2,1)S(1)} %get-tuple-element.4) | data formatting | bytes 1048576
  51.2 0.6 %copy.14 = f32[64,64]{1,0:T(8,128)} copy(f32[64,64]{1,0:T(8,128)S(1)} %get-tuple-element.5) | data formatting | bytes 32768
Async XLA Ops:
  3.2 1.0 %copy-start = (bf16[64,4096]{1,0:T(8,128)(2,1)S(1)}, bf16[64,4096]{1,0:T(8,128)(2,1)}, u32[]{:S(2)}) copy-start(bf16[64,4096]{1,0:T(8,128)(2,1)} %val.1) | copy-start | bytes 1572868
  4.2 0.7 %copy-start.1 = (s32[64]{0:T(128)S(1)}, s32[64]{0:T(128)}, u32[]{:S(2)}) copy-start(s32[64]{0:T(128)} %param.12) | copy-start | bytes 772
  4.9 0.7 %copy-start.2 = (s32[64]{0:T(128)S(1)}, s32[64]{0:T(128)}, u32[]{:S(2)}) copy-start(s32[64]{0:T(128)} %ids.1) | copy-start | bytes 772

commit v2 on v1

--- a/solution.py
+++ b/solution.py
@@ -19,16 +19,16 @@
 
 
 def kernel(
-    size, slots, act, grads, basis_in, basis_out, val, owner, ids, sketches, scores,
-    abuf, gbuf, wide_in, wide_out, sent, xbuf, zbuf, acc, terms, firsts, held, pieces,
-    act_sem, grad_sem, x_send, x_recv, z_send, z_recv, first_send, first_recv,
+    size, slots, act, grads, basis_in, basis_out, val_hbm, owner_hbm, ids_hbm, sketches, scores,
+    abuf, gbuf, val, owner, ids, wide_in, wide_out, sent, xbuf, zbuf, acc, terms, firsts, held, pieces,
+    act_sem, grad_sem, in_sem, out_sem, val_sem, owner_sem, ids_sem, x_send, x_recv, z_send, z_recv, first_send, first_recv,
     gx_send, gz_send, gc_send, g_recv, s_send, s_recv,
 ):
     c = lax.axis_index("context")
     t = lax.axis_index("tensor")
     half = size // 2
     rows = acc.shape[0]
-    rank = basis_in.shape[1]
+    rank = basis_in.shape[0]
     examples = sketches.shape[0]
     parity, mine = t % 2, t // 2
     pair = t + 1 - 2 * parity
@@ -37,11 +37,20 @@
     block = rows * size // nblock
 
     def peer(j):
-        return (mine + 1 + j) % half
+        flip, result, bit = half - 1 - j, 0, 1
+        while bit < half:
+            result = result + (mine // bit + flip // bit) % 2 * bit
+            bit = bit * 2
+        return result
+
+    def near(i):
+        return (i == size - 1) | ((i > 0) & (i % 2 == 0))
+
+    def place(i):
+        return jnp.where(i == size - 1, half - 1, jnp.where(near(i), (i + size - 2) // 2 % half, (i + 1) // 2))
 
     def target(i):
-        side = jnp.where(i < half, 1 - parity, parity)
-        return 2 * peer(i % half) + side
+        return 2 * peer(place(i)) + jnp.where(near(i), parity, 1 - parity)
 
     def load(i):
         slot = i % BUFFERS
@@ -55,6 +64,18 @@
         for copy in load(i):
             copy.start()
 
+    fixed = (
+        pltpu.make_async_copy(basis_in, wide_in.at[:rank], in_sem),
+        pltpu.make_async_copy(basis_out, wide_out.at[rank:], out_sem),
+    )
+    stored = (
+        pltpu.make_async_copy(val_hbm, val, val_sem),
+        pltpu.make_async_copy(owner_hbm, owner, owner_sem),
+    )
+    labels = pltpu.make_async_copy(ids_hbm, ids, ids_sem)
+    labels.start()
+    for copy in fixed:
+        copy.start()
     for i in range(BUFFERS - 1):
         begin(i)
 
@@ -67,11 +88,10 @@
     lax.fori_loop(0, size - 1, greet, 0)
     pl.semaphore_signal(barrier, inc=1, device_id={"context": other}, device_id_type=MESH)
 
-    wide_in[...] = jnp.zeros_like(wide_in)
-    wide_out[...] = jnp.zeros_like(wide_out)
-    wide_in[:, :rank] = basis_in[...]
-    wide_out[:, rank:] = basis_out[...]
-
+    wide_in[rank:] = jnp.zeros((rank, wide_in.shape[1]), BF16)
+    wide_out[:rank] = jnp.zeros((rank, wide_out.shape[1]), BF16)
+
+    labels.wait()
     lanes = firsts.shape[2]
     lane = lax.broadcasted_iota(jnp.int32, (8, lanes), 1)
 
@@ -79,7 +99,6 @@
         return jnp.where(lane // (2 * slots) == j, ids[(j * rows) // block], vector)
 
     firsts[c] = lax.fori_loop(0, size, first, jnp.zeros((8, lanes), jnp.int32))
-    pl.semaphore_wait(barrier, size)
 
     def share_firsts(index):
         return pltpu.make_async_remote_copy(
@@ -87,7 +106,9 @@
             device_id={"context": other}, device_id_type=MESH,
         )
 
-    share_firsts(c).start()
+    for copy in fixed:
+        copy.wait()
+    turned = (((1,), (1,)), ((), ()))
 
     def project(i):
         slot = i % BUFFERS
@@ -98,8 +119,8 @@
         def _():
             begin(i + BUFFERS - 1)
 
-        return jnp.dot(abuf[slot], wide_in[...], preferred_element_type=F32) + jnp.dot(
-            gbuf[slot], wide_out[...], preferred_element_type=F32
+        return lax.dot_general(abuf[slot], wide_in[...], turned, preferred_element_type=F32) + lax.dot_general(
+            gbuf[slot], wide_out[...], turned, preferred_element_type=F32
         )
 
     def across(k):
@@ -114,29 +135,36 @@
             device_id={"tensor": 2 * k + parity}, device_id_type=MESH,
         )
 
-    def first_half(i, carry):
-        k = peer(i)
-        sent[k] = project(i).astype(BF16)
-        across(k).start()
+    def chunk(i, carry):
+        k = peer(place(i))
+        value = project(i)
+
+        @pl.when(i == 0)
+        def _():
+            pl.semaphore_wait(barrier, size)
+            share_firsts(c).start()
+
+        @pl.when(jnp.logical_not(near(i)))
+        def _():
+            sent[k] = value.astype(BF16)
+            across(k).start()
+
+        @pl.when(near(i))
+        def _():
+            across(k).wait_recv()
+            total = value + xbuf[k].astype(F32)
+            acc[...] = total
+
+            @pl.when(i < size - 1)
+            def _():
+                sent[half + k] = total.astype(BF16)
+                along(k, mine).start()
+
         return carry
 
-    lax.fori_loop(0, half, first_half, 0)
-
-    def second_half(i, carry):
-        k = peer(i)
-        value = project(half + i)
-        across(k).wait_recv()
-        value = value + xbuf[k].astype(F32)
-        acc[...] = value
-
-        @pl.when(i < half - 1)
-        def _():
-            sent[half + k] = value.astype(BF16)
-            along(k, mine).start()
-
-        return carry
-
-    lax.fori_loop(0, half, second_half, 0)
+    lax.fori_loop(0, size, chunk, 0)
+    for copy in stored:
+        copy.start()
 
     def collect(j, carry):
         k = peer(j)
@@ -241,9 +269,9 @@
         sketches[:, p * tile:(p + 1) * tile] = total[:examples]
         sketches[:, wide + p * tile:wide + (p + 1) * tile] = total[examples:]
 
-    local = lax.dot_general(
-        val[...], sketches[...], (((1,), (1,)), ((), ())), preferred_element_type=F32
-    )
+    for copy in stored:
+        copy.wait()
+    local = lax.dot_general(val[...], sketches[...], turned, preferred_element_type=F32)
     depth = pieces.shape[1]
     pieces[t] = jnp.concatenate([local[:depth], local[depth:]], axis=1)
 
@@ -309,7 +337,7 @@
     else:
         val_owner_at = val_owner
     vmem = pl.BlockSpec(memory_space=pltpu.VMEM)
-    hbm = pl.BlockSpec(memory_space=pl.ANY)
+    hbm = pl.BlockSpec(memory_space=pltpu.HBM)
     dma = pltpu.SemaphoreType.DMA
     return pl.pallas_call(
         functools.partial(kernel, size, slots),
@@ -317,13 +345,16 @@
             jax.ShapeDtypeStruct((examples, width), BF16),
             jax.ShapeDtypeStruct((examples, stored), F32),
         ),
-        in_specs=[hbm, hbm, vmem, vmem, vmem, vmem, pl.BlockSpec(memory_space=pltpu.SMEM)],
+        in_specs=[hbm] * 7,
         out_specs=(vmem, vmem),
         scratch_shapes=[
             pltpu.VMEM((BUFFERS, rows, deep_in), BF16),
             pltpu.VMEM((BUFFERS, rows, deep_out), BF16),
-            pltpu.VMEM((deep_in, 2 * rank), BF16),
-            pltpu.VMEM((deep_out, 2 * rank), BF16),
+            pltpu.VMEM((2 * depth, width), BF16),
+            pltpu.VMEM((1, stored), jnp.int32),
+            pltpu.SMEM((nblock,), jnp.int32),
+            pltpu.VMEM((2 * rank, deep_in), BF16),
+            pltpu.VMEM((2 * rank, deep_out), BF16),
             pltpu.VMEM((size, rows, 2 * rank), BF16),
             pltpu.VMEM((half, rows, 2 * rank), BF16),
             pltpu.VMEM((half, rows, 2 * rank), BF16),
@@ -332,7 +363,7 @@
             pltpu.VMEM((2, 8, size * 2 * slots), jnp.int32),
             pltpu.VMEM((2 * size, 2 * slots, width // 2), BF16),
             pltpu.VMEM((size, depth, 2 * examples), F32),
-            dma((BUFFERS,)), dma((BUFFERS,)),
+            dma((BUFFERS,)), dma((BUFFERS,)), dma, dma, dma, dma, dma,
             dma((half,)), dma((half,)), dma((half,)), dma((half,)),
             dma, dma,
             dma((half,)), dma((half,)), dma((size,)), dma((2 * size,)),
@@ -346,7 +377,7 @@
             bytes_accessed=2 * tokens * (deep_in + deep_out),
             transcendentals=0,
         ),
-    )(activations, out_grads, basis_in, basis_out, val_sketches, val_owner_at.reshape(1, stored), example_ids)
+    )(*[pltpu.with_memory_space_constraint(x, pltpu.HBM) for x in (activations, out_grads, basis_in.T, basis_out.T, val_sketches, val_owner_at.reshape(1, stored), example_ids)])
 
 
 def solution(mesh):

time: 52 us -> 43.3 us (0.83)
  local copies, waits for them, and re-layouts: 6.28 us -> 1.41 us
  Pallas kernels: 44.9 us -> 41.1 us
    unnamed x10 -> x2, local copies, waits for them, and re-layouts: 6.28 us -> 1.41 us
    pallas_call x1, Pallas kernels: 44.9 us -> 41.1 us  [per_device(): pl.pallas_call(functools.partial(kernel, size, slots), out_shape=(jax.Sha...]
where the time goes in v2:
time: 43.3 us; the launch traced here: 43.1 us
  Pallas kernels  41.1 us (95%)
  local copies, waits for them, and re-layouts  1.41 us (3%)
  between operations  0.64 us (1%)
    pallas_call x1, Pallas kernels, per_device(): pl.pallas_call(functools.partial(kernel, size, slots), out_shape=(jax.Sha...  41.1 us
    unnamed x2, local copies, waits for them, and re-layouts  1.41 us

profile of v2, /device:TPU:1, one launch (start us, length us, event | category | flops | bytes accessed | tf_op | source)
XLA Modules:
  0.0 43.1 jit_solution(458053365486132500)
XLA Ops:
  0.6 41.1 %shard_map.86 = (bf16[64,4096]{1,0:T(8,128)(2,1)S(1)}, f32[64,64]{1,0:T(8,128)S(1)}) custom-call(bf16[4096,3584]{1,0:T(8,128)(2,1)} %act.1, bf16[4096,1024]{1,0:T(8,128)(2,1)} %grads.1, bf16[64,3584]{1,0:T(8,128)(2,1)} %bitcast.3, bf16[64,1024]{1,0:T(8,128)(2,1)} %bitcast.4, bf16[64,4096]{1,0:T(8,128)(2,1)} %val_hbm.1, s32[1,64]{1,0:T(1,128)} %bitcast.5, ...), custom_call_target="tpu_custom_call" | custom-call | flops 2415919104 | bytes 37748736 | tf_op jit(solution)/shard_map/pallas_call | solution.py:342
  41.7 0.8 %copy.11 = bf16[64,4096]{1,0:T(8,128)(2,1)} copy(bf16[64,4096]{1,0:T(8,128)(2,1)S(1)} %get-tuple-element.4) | data formatting | bytes 1048576
  42.5 0.6 %copy.12 = f32[64,64]{1,0:T(8,128)} copy(f32[64,64]{1,0:T(8,128)S(1)} %get-tuple-element.5) | data formatting | bytes 32768

commit v3 on v2

--- a/solution.py
+++ b/solution.py
@@ -217,6 +217,9 @@
     def to_pair(k):
         return give(c * size + 2 * k + parity, gx_send.at[k], {"tensor": pair})
 
+    def to_diagonal():
+        return give(me, gx_send.at[peer(half - 2)], {"tensor": 2 * peer(half - 2) + 1 - parity})
+
     def to_core(k):
         return give(c * size + k, gc_send.at[k], {"context": other})
 
@@ -232,18 +235,24 @@
 
     loop(half - 1, lambda j: to_peer(peer(j)).start())
     to_pair(mine).start()
+    if half > 1:
+        to_diagonal().start()
     to_core(t).start()
 
     def from_peer(j):
         k = peer(j)
         arrived(c * size + 2 * k + parity)
-        to_pair(k).start()
+
+        @pl.when(j < half - 2)
+        def _():
+            to_pair(k).start()
+
         to_core(2 * k + parity).start()
 
     loop(half - 1, from_peer)
 
     def from_pair(j):
-        k = 2 * peer(half - 1 + j) + 1 - parity
+        k = 2 * peer((half - 1 + j) % half) + 1 - parity
         arrived(c * size + k)
         to_core(k).start()
 
@@ -314,7 +323,10 @@
     loop(half, lambda k: across(k).wait_send())
     loop(half - 1, lambda j: along(peer(j), mine).wait_send())
     loop(half - 1, lambda j: to_peer(peer(j)).wait_send())
-    loop(half, lambda k: to_pair(k).wait_send())
+    loop(half - 2, lambda j: to_pair(peer(j)).wait_send())
+    to_pair(mine).wait_send()
+    if half > 1:
+        to_diagonal().wait_send()
     loop(size, lambda k: to_core(k).wait_send())
     loop(size - 1, lambda j: send_scores((t + 1 + j) % size, t).wait_send())
 

time: 43.3 us -> 42.8 us (0.988)
  Pallas kernels: 41.1 us -> 40.6 us
    pallas_call x1, Pallas kernels: 41.1 us -> 40.6 us  [per_device(): pl.pallas_call(functools.partial(kernel, size, slots), out_shape=(jax.Sha...]
where the time goes in v3:
time: 42.8 us; the launch traced here: 42.6 us
  Pallas kernels  40.6 us (95%)
  local copies, waits for them, and re-layouts  1.41 us (3%)
  between operations  0.64 us (1%)
    pallas_call x1, Pallas kernels, per_device(): pl.pallas_call(functools.partial(kernel, size, slots), out_shape=(jax.Sha...  40.6 us
    unnamed x2, local copies, waits for them, and re-layouts  1.41 us

profile of v3, /device:TPU:1, one launch (start us, length us, event | category | flops | bytes accessed | tf_op | source)
XLA Modules:
  0.0 42.6 jit_solution(11025418613946588345)
XLA Ops:
  0.6 40.6 %shard_map.86 = (bf16[64,4096]{1,0:T(8,128)(2,1)S(1)}, f32[64,64]{1,0:T(8,128)S(1)}) custom-call(bf16[4096,3584]{1,0:T(8,128)(2,1)} %act.1, bf16[4096,1024]{1,0:T(8,128)(2,1)} %grads.1, bf16[64,3584]{1,0:T(8,128)(2,1)} %bitcast.3, bf16[64,1024]{1,0:T(8,128)(2,1)} %bitcast.4, bf16[64,4096]{1,0:T(8,128)(2,1)} %val_hbm.1, s32[1,64]{1,0:T(1,128)} %bitcast.5, ...), custom_call_target="tpu_custom_call" | custom-call | flops 2415919104 | bytes 37748736 | tf_op jit(solution)/shard_map/pallas_call | solution.py:354
  41.2 0.8 %copy.11 = bf16[64,4096]{1,0:T(8,128)(2,1)} copy(bf16[64,4096]{1,0:T(8,128)(2,1)S(1)} %get-tuple-element.4) | data formatting | bytes 1048576
  42.0 0.6 %copy.12 = f32[64,64]{1,0:T(8,128)} copy(f32[64,64]{1,0:T(8,128)S(1)} %get-tuple-element.5) | data formatting | bytes 32768

commit v4 on v3

--- a/solution.py
+++ b/solution.py
@@ -44,10 +44,10 @@
         return result
 
     def near(i):
-        return (i == size - 1) | ((i > 0) & (i % 2 == 0))
+        return (i >= size - 2) | ((i >= 3) & (i % 2 == 1))
 
     def place(i):
-        return jnp.where(i == size - 1, half - 1, jnp.where(near(i), (i + size - 2) // 2 % half, (i + 1) // 2))
+        return jnp.where(i >= size - 2, i - half, jnp.where(near(i), (i - 3) // 2 % half, jnp.where(i < 2, i, i // 2 + 1)))
 
     def target(i):
         return 2 * peer(place(i)) + jnp.where(near(i), parity, 1 - parity)

time: 42.8 us -> 42.9 us (level)
  no operation moved by 1% of the time
where the time goes in v4:
time: 42.9 us; the launch traced here: 42.7 us
  Pallas kernels  40.7 us (95%)
  local copies, waits for them, and re-layouts  1.41 us (3%)
  between operations  0.64 us (1%)
    pallas_call x1, Pallas kernels, per_device(): pl.pallas_call(functools.partial(kernel, size, slots), out_shape=(jax.Sha...  40.7 us
    unnamed x2, local copies, waits for them, and re-layouts  1.41 us

profile of v4, /device:TPU:1, one launch (start us, length us, event | category | flops | bytes accessed | tf_op | source)
XLA Modules:
  0.0 42.7 jit_solution(1915975647001314091)
XLA Ops:
  0.6 40.7 %shard_map.86 = (bf16[64,4096]{1,0:T(8,128)(2,1)S(1)}, f32[64,64]{1,0:T(8,128)S(1)}) custom-call(bf16[4096,3584]{1,0:T(8,128)(2,1)} %act.1, bf16[4096,1024]{1,0:T(8,128)(2,1)} %grads.1, bf16[64,3584]{1,0:T(8,128)(2,1)} %bitcast.3, bf16[64,1024]{1,0:T(8,128)(2,1)} %bitcast.4, bf16[64,4096]{1,0:T(8,128)(2,1)} %val_hbm.1, s32[1,64]{1,0:T(1,128)} %bitcast.5, ...), custom_call_target="tpu_custom_call" | custom-call | flops 2415919104 | bytes 37748736 | tf_op jit(solution)/shard_map/pallas_call | solution.py:354
  41.3 0.8 %copy.11 = bf16[64,4096]{1,0:T(8,128)(2,1)} copy(bf16[64,4096]{1,0:T(8,128)(2,1)S(1)} %get-tuple-element.4) | data formatting | bytes 1048576
  42.1 0.6 %copy.12 = f32[64,64]{1,0:T(8,128)} copy(f32[64,64]{1,0:T(8,128)S(1)} %get-tuple-element.5) | data formatting | bytes 32768
